TPU v7x, 512 devices: a whole 4x4x16 slice. The times are simulated.
512 devices in a mesh: rows: 64 (over y, z), rep: 8 (over x, core).
Axes of the slice: x: 4, y: 4, z: 16, core: 2. Of those that a mesh axis runs over, the one named last changes fastest.
Arguments:
- features: bfloat16 [65536, 512], P('rows', 'rep'), may hold values from -6 to 6
- neighbor_blocks: int32 [512, 2], P('rows'), may hold values from 0 to 511, as said below
- adjacency: bfloat16 [512, 2, 128, 128], P('rows'), may hold values from 0 to 100, as said below
- w_self: bfloat16 [512, 512], replicated, may hold values from -0.25 to 0.25
- w_neigh: bfloat16 [512, 512], replicated, may hold values from -0.25 to 0.25
- cotangent: bfloat16 [65536, 512], P(('rows', 'rep')), may hold values from -0.09375 to 0.09375
Outputs:
- output: bfloat16 [65536, 512], P(('rows', 'rep'))
- weight_grads: float32 [2, 512, 512], P(None, 'rows', 'rep')
Inputs may be any that keep to these rules, and one draw needn't show every extreme that they name: `neighbor_blocks`: column block c belongs to index c // 8 of rows. Over the 16 entries of one index of rows, no index of rows is named more than 2 times, and some index of rows is named exactly 2 times by every index of rows. `adjacency`: entries are zero or positive.
All inputs are finite; a program needn't handle non-finite values.
Results may differ from a plain program's by a relative error of at most 0.006.
Values may be sent and summed in bfloat16 or wider, within the bound.
A program may use at most 64 MiB of HBM per device.

v0:
```python
import jax
import jax.numpy as jnp
from jax import lax
from jax.sharding import PartitionSpec as P


def silu_slope(pre_act):
    gate_value = jax.nn.sigmoid(pre_act)
    return gate_value * (1.0 + pre_act * (1.0 - gate_value))


def local(features, neighbor_blocks, adjacency, w_self, w_neigh, cotangent):
    row_count = lax.axis_size("rows")
    row_blocks, per_block, block_size, _ = adjacency.shape
    node_here, slice_width = features.shape
    use_count = row_blocks * per_block
    capacity = max(2, (2 * use_count + row_count - 1) // row_count)
    wanted = neighbor_blocks.reshape(use_count)
    owners = wanted // row_blocks
    local_ids = wanted % row_blocks
    owner_match = (owners[:, None] == jnp.arange(row_count, dtype=jnp.int32)[None, :]).astype(
        jnp.int32
    )
    use_rank = jnp.sum((jnp.cumsum(owner_match, axis=0) - 1) * owner_match, axis=1)
    slot_ids = owners * capacity + use_rank
    slot_match = (
        slot_ids[:, None] == jnp.arange(row_count * capacity, dtype=jnp.int32)[None, :]
    ).astype(jnp.int32)
    request_table = jnp.sum(slot_match * local_ids[:, None], axis=0).reshape(row_count, capacity)
    incoming = lax.all_to_all(request_table, "rows", split_axis=0, concat_axis=0, tiled=True)
    feature_tiles = features.reshape(row_blocks, block_size, slice_width)
    outgoing = jnp.take(feature_tiles, incoming.reshape(row_count * capacity), axis=0)
    outgoing = outgoing.reshape(row_count, capacity, block_size, slice_width)
    weights_flat = adjacency.reshape(use_count, block_size, block_size)
    totals = jnp.sum(adjacency, axis=(1, 3), dtype=jnp.float32).reshape(node_here)
    row_scale = 1.0 / jnp.sqrt(1.0 + totals)
    received = lax.all_to_all(outgoing, "rows", split_axis=0, concat_axis=0, tiled=True)
    stacked = received.reshape(row_count * capacity, block_size, received.shape[3])
    picked = jnp.take(stacked, slot_ids, axis=0)
    raw_sum = jnp.einsum("uij,ujf->uif", weights_flat, picked, preferred_element_type=jnp.float32)
    raw_agg = jnp.sum(raw_sum.reshape(row_blocks, per_block, block_size, -1), axis=1).reshape(
        node_here, -1
    )
    agg_slice = (row_scale[:, None] * raw_agg).astype(jnp.bfloat16)
    own_features, own_agg = (
        lax.all_to_all(features, "rep", split_axis=0, concat_axis=1, tiled=True),
        lax.all_to_all(agg_slice, "rep", split_axis=0, concat_axis=1, tiled=True),
    )
    self_term = jnp.dot(own_features, w_self, preferred_element_type=jnp.float32)
    pre_act = self_term + jnp.dot(own_agg, w_neigh, preferred_element_type=jnp.float32)
    output = jax.nn.silu(pre_act).astype(jnp.bfloat16)
    grad_pre = (cotangent.astype(jnp.float32) * silu_slope(pre_act)).astype(jnp.bfloat16)
    grad_self = jnp.einsum("nf,ng->fg", own_features, grad_pre, preferred_element_type=jnp.float32)
    grad_neigh = jnp.einsum("nf,ng->fg", own_agg, grad_pre, preferred_element_type=jnp.float32)
    partial_grads = jnp.stack([grad_self, grad_neigh])
    reduced = lax.psum_scatter(partial_grads, "rows", scatter_dimension=1, tiled=True)
    weight_grads = lax.psum_scatter(reduced, "rep", scatter_dimension=2, tiled=True)
    return (output, weight_grads)


def solution(mesh):
    in_specs = (
        P("rows", "rep"),
        P("rows", None),
        P("rows", None, None, None),
        P(),
        P(),
        P(("rows", "rep"), None),
    )
    out_specs = (P(("rows", "rep"), None), P(None, "rows", "rep"))
    return jax.shard_map(local, mesh=mesh, in_specs=in_specs, out_specs=out_specs, check_vma=False)
```

profile of v0, /device:TPU:6, one launch (start us, length us, event | category | flops | bytes accessed | tf_op | source)
XLA Modules:
  0.0 484.8 jit_solution(7894905705934835121)
XLA Ops:
  7.2 0.0 copy-start
  7.2 0.8 copy.49
  8.0 0.1 reshape.223
  8.1 0.1 fusion.6
  8.2 0.2 select_reduce_fusion.1
  8.4 0.1 select_reduce_fusion
  8.5 0.7 all_to_all.39
  9.2 18.7 %all-to-all-start.1 = ((s32[64,1,2]{2,1,0:T(1,128)}), s32[64,1,2]{2,1,0:T(1,128)S(1)}, u32[]{:S(2)}, u32[]{:S(2)}) async-start(s32[64,1,2]{2,1,0:T(1,128)} %bitcast.2), calls=%async_computation.1 | async-start | bytes 65536 | tf_op jit(solution)/shard_map/all_to_all | solution.py:30
  28.0 1.6 copy_bitcast_fusion
  29.6 12.7 %all-to-all-done.1 = s32[64,1,2]{2,1,0:T(1,128)S(1)} async-done(((s32[64,1,2]{2,1,0:T(1,128)}), s32[64,1,2]{2,1,0:T(1,128)S(1)}, u32[]{:S(2)}, u32[]{:S(2)}) %all-to-all-start.1) | async-done | bytes 544 | tf_op jit(solution)/shard_map/all_to_all | solution.py:30
  42.2 0.5 broadcast.279
  42.8 0.7 reduce.3
  43.5 0.1 reshape.225
  43.6 0.1 copy.51
  43.7 0.1 copy.52
  43.9 1.9 gather_fusion
  45.7 1.6 broadcast_select_fusion
  47.3 0.0 copy-start.1
  47.3 4.8 all-to-all-start.2
  52.2 0.1 reshape.227
  52.3 0.0 copy-done.1
  52.3 0.2 convert_reduce_fusion
  52.5 96.9 %all-to-all-done.2 = bf16[64,2,128,64]{2,3,1,0:T(8,128)(2,1)S(1)} async-done(((bf16[64,2,128,64]{2,3,1,0:T(8,128)(2,1)}), bf16[64,2,128,64]{2,3,1,0:T(8,128)(2,1)S(1)}, u32[]{:S(2)}, u32[]{:S(2)}) %all-to-all-start.2) | async-done | bytes 2097184 | tf_op jit(solution)/shard_map/all_to_all | solution.py:37
  149.4 4.8 all-to-all-start
  154.2 0.6 gather_fusion.1
  154.8 0.0 copy-start.2
  154.8 0.5 bitcast_reduce_fusion
  155.3 0.7 multiply_convert_fusion.2
  156.0 2.3 all-to-all-done
  158.3 5.4 %all-to-all-start.3 = ((bf16[8,128,64]{1,2,0:T(8,128)(2,1)}), bf16[8,128,64]{1,2,0:T(8,128)(2,1)S(1)}, u32[]{:S(2)}, u32[]{:S(2)}) async-start(bf16[8,128,64]{1,2,0:T(8,128)(2,1)} %multiply_convert_fusion.2), calls=%async_computation.3 | async-start | bytes 262144 | tf_op jit(solution)/shard_map/all_to_all | solution.py:47
  163.7 0.0 all-reduce.3.cloned.1.call-start
  163.7 1.3 fusion.10
  165.0 2.7 all-to-all-done.3
  167.7 0.0 copy-done
  167.7 1.0 multiply_convert_fusion.1
  168.7 0.0 copy-done.2
  168.7 0.4 convolution_bitcast_fusion
  169.0 0.3 convolution_bitcast_fusion.1
  169.4 0.2 pad_maximum_fusion
  169.6 2.5 copy.56
  172.0 0.0 all-reduce.3.cloned.1.call-update
  172.0 0.0 reduce-scatter.4.cloned.1.call-start
  172.1 1.3 dynamic-slice
  174.0 269.1 %all-reduce.3.cloned.1.call-done = f32[2,512,512]{2,0,1:T(2,128)} async-done(((f32[2,512,512]{2,0,1:T(2,128)}), f32[2,512,512]{2,0,1:T(2,128)}) %all-reduce.3.cloned.1.call-update) | async-done | bytes 2097168
  443.1 0.8 constant_dynamic-slice_fusion
  443.9 0.8 copy.59
  444.7 1.2 reshape.246
  445.9 0.0 reduce-scatter.4.cloned.1.call-update
  446.0 30.4 %reduce-scatter.4.cloned.1.call-done = f32[64,16]{1,0:T(8,128)} async-done(((f32[512,16]{1,0:T(8,128)}), f32[64,16]{1,0:T(8,128)}) %reduce-scatter.4.cloned.1.call-update) | async-done | bytes 4112
  476.4 0.9 reshape.247
  477.2 0.7 copy.57
  (9 shorter events, 0.1 us)
Async XLA Ops:
  7.2 160.5 %copy-start = (bf16[512,512]{1,0:T(8,128)(2,1)S(1)}, bf16[512,512]{1,0:T(8,128)(2,1)}, u32[]{:S(2)}) copy-start(bf16[512,512]{1,0:T(8,128)(2,1)} %param.10) | copy-start | bytes 1572868
  9.2 33.0 %all-to-all-start.1 = ((s32[64,1,2]{2,1,0:T(1,128)}), s32[64,1,2]{2,1,0:T(1,128)S(1)}, u32[]{:S(2)}, u32[]{:S(2)}) async-start(s32[64,1,2]{2,1,0:T(1,128)} %bitcast.2), calls=%async_computation.1 | async-start | bytes 65536 | tf_op jit(solution)/shard_map/all_to_all | solution.py:30
  47.3 4.9 %copy-start.1 = (bf16[8,2,128,128]{3,2,1,0:T(8,128)(2,1)S(1)}, bf16[8,2,128,128]{3,2,1,0:T(8,128)(2,1)}, u32[]{:S(2)}) copy-start(bf16[8,2,128,128]{3,2,1,0:T(8,128)(2,1)} %param.8) | copy-start | bytes 1572868
  47.3 102.1 %all-to-all-start.2 = ((bf16[64,2,128,64]{2,3,1,0:T(8,128)(2,1)}), bf16[64,2,128,64]{2,3,1,0:T(8,128)(2,1)S(1)}, u32[]{:S(2)}, u32[]{:S(2)}) async-start(bf16[64,2,128,64]{2,3,1,0:T(8,128)(2,1)} %broadcast_select_fusion), calls=%async_computation.2 | async-start | bytes 4194304 | tf_op jit(solution)/shard_map/all_to_all | solution.py:37
  149.4 8.8 %all-to-all-start = ((bf16[8,128,64]{1,2,0:T(8,128)(2,1)}), bf16[8,128,64]{1,2,0:T(8,128)(2,1)S(1)}, u32[]{:S(2)}, u32[]{:S(2)}) async-start(bf16[8,128,64]{1,2,0:T(8,128)(2,1)} %copy_bitcast_fusion), calls=%async_computation | async-start | bytes 262144 | tf_op jit(solution)/shard_map/all_to_all | solution.py:46
  154.8 13.9 %copy-start.2 = (bf16[128,512]{1,0:T(8,128)(2,1)S(1)}, bf16[128,512]{1,0:T(8,128)(2,1)}, u32[]{:S(2)}) copy-start(bf16[128,512]{1,0:T(8,128)(2,1)} %param.11) | copy-start | bytes 393220
  158.3 9.4 %all-to-all-start.3 = ((bf16[8,128,64]{1,2,0:T(8,128)(2,1)}), bf16[8,128,64]{1,2,0:T(8,128)(2,1)S(1)}, u32[]{:S(2)}, u32[]{:S(2)}) async-start(bf16[8,128,64]{1,2,0:T(8,128)(2,1)} %multiply_convert_fusion.2), calls=%async_computation.3 | async-start | bytes 262144 | tf_op jit(solution)/shard_map/all_to_all | solution.py:47
  163.7 279.5 %all-reduce.3.cloned.1.call-start = ((), (), s32[]{:S(2)}) async-start(), calls=%async_computation.6 | async-start | bytes 4194304
  172.0 304.3 %reduce-scatter.4.cloned.1.call-start = ((), (), s32[]{:S(2)}) async-start(), calls=%async_computation.5 | async-start | bytes 294912
Sparse Core Ops, SparseCore 0:
  172.2 270.9 all-reduce.2
  446.2 30.1 reduce-scatter.3
where the time goes:
time: 488 us; the launch traced here: 485 us
  waiting for transfers between devices  414 us (85%)
  starting transfers between devices  33.7 us (7%)
  local copies, waits for them, and re-layouts  14.8 us (3%)
  between operations  14.8 us (3%)
    unnamed x4, waiting for transfers between devices  300 us
    all_to_all x1, waiting for transfers between devices, local(): lax.all_to_all(outgoing, 'rows', split_axis=0, concat_axis=0, tiled=True)  96.9 us
    all_to_all x1, starting transfers between devices, local(): lax.all_to_all(request_table, 'rows', split_axis=0, concat_axis=0, tiled=...  18.7 us
    all_to_all x1, waiting for transfers between devices, local(): lax.all_to_all(request_table, 'rows', split_axis=0, concat_axis=0, tiled=...  12.7 us
  transfers between devices with their start and end apart: 6, of which 6 were waited for; matrix products, arithmetic and copies ran while one was open for 1% of the time, Pallas kernels for 0%

commit v1 on v0

v1 whole, which is shorter than its diff:
```python
import jax
import jax.numpy as jnp
from jax import lax
from jax.experimental import pallas as pl
from jax.experimental.pallas import tpu as pltpu
from jax.sharding import PartitionSpec as P

Y, Z, X = 4, 16, 4
REP = 2 * X
SUB = 4
PIECE = 8 // SUB
HALF = Z // 2
MESH = pl.DeviceIdType.MESH
BF, F32 = jnp.bfloat16, jnp.float32


def dot(a, b, ca, cb):
    return lax.dot_general(a, b, (((ca,), (cb,)), ((), ())), preferred_element_type=F32)


def kernel(
    nb_ref, f_hbm, adj_hbm, ws_hbm, wn_hbm, cot_hbm,
    out_ref, wg_ref,
    zbuf, far_out, far_in, near_out, near_in, own_f, own_a, lhs, adj, ws, wn, cot,
    scale, pre_self, g_own, g_all, parts, y_in, y_sum, z_in, nb_all, nb_s,
    load_sem, zs, zr, fs, fr, as_, ar, gs, gr, ps, pr, ns, nr, ys, yr, ts, tr, us, ur,
):
    row, rep = lax.axis_index("rows"), lax.axis_index("rep")
    y, z = row // Z, lax.rem(row, Z)
    x, core = rep // 2, lax.rem(rep, 2)

    def in_rows(yy, zz):
        return {"rows": yy * Z + zz, "rep": rep}

    def in_rep(q):
        return {"rows": row, "rep": q}

    def remote(src, dst, send, recv, device):
        return pltpu.make_async_remote_copy(
            src_ref=src, dst_ref=dst, send_sem=send, recv_sem=recv,
            device_id=device, device_id_type=MESH,
        )

    def turn(a, k, n):
        return lax.rem(a + k + n, n)

    right, left = in_rows(y, turn(z, 1, Z)), in_rows(y, turn(z, -1, Z))
    y_next, y_prev, y_far = turn(y, 1, Y), turn(y, -1, Y), turn(y, 2, Y)

    first = [
        pltpu.make_async_copy(
            f_hbm.at[:, pl.ds(128 * l, 128)], zbuf.at[z * 8 + l], load_sem.at[l]
        )
        for l in range(8)
    ]
    mine = pl.ds(pl.multiple_of(core * 64, 64), 64)
    mine_a = pl.ds(pl.multiple_of(128 + core * 64, 64), 64)
    later = [
        pltpu.make_async_copy(f_hbm, lhs.at[mine], load_sem.at[8]),
        pltpu.make_async_copy(adj_hbm, adj, load_sem.at[9]),
        pltpu.make_async_copy(ws_hbm, ws, load_sem.at[10]),
        pltpu.make_async_copy(wn_hbm, wn, load_sem.at[11]),
        pltpu.make_async_copy(cot_hbm, cot, load_sem.at[12]),
    ]
    for c in first + later:
        c.start()

    barrier = pltpu.get_barrier_semaphore()
    for device in (right, left):
        pl.semaphore_signal(barrier, inc=1, device_id=device, device_id_type=MESH)
    for k in range(1, Y):
        pl.semaphore_signal(
            barrier, inc=1, device_id=in_rows(turn(y, k, Y), z), device_id_type=MESH
        )
    for k in range(1, REP):
        pl.semaphore_signal(
            barrier, inc=1, device_id=in_rep(turn(rep, k, REP)), device_id_type=MESH
        )
    nb_all[y] = nb_ref[...]
    for c in first:
        c.wait()
    pl.semaphore_wait(barrier, 2 + (Y - 1) + (REP - 1))

    def ring_copy(way, step, piece, chunk):
        at = pl.ds(chunk * 8 + piece * PIECE, PIECE)
        return remote(
            zbuf.at[at], zbuf.at[at], zs.at[way, step, piece], zr.at[way, step, piece],
            right if way == 0 else left,
        )

    def sent(way, step, piece):
        return ring_copy(way, step, piece, turn(z, -step if way == 0 else step, Z))

    def arriving(way, step, piece):
        return ring_copy(way, step, piece, turn(z, -1 - step if way == 0 else 1 + step, Z))

    def last_way(piece):
        return 0 if piece < SUB // 2 else 1

    for piece in range(SUB):
        for way in range(2):
            sent(way, 0, piece).start()

    def feature_copy(k, q, source):
        return remote(
            zbuf.at[z * 8 + q], own_f.at[pl.ds(pl.multiple_of(source * 64, 64), 64)],
            fs.at[k - 1], fr.at[k - 1], in_rep(q),
        )

    def nb_copy(k, source):
        return remote(
            nb_all.at[source], nb_all.at[source], ns.at[k - 1], nr.at[k - 1],
            in_rows(turn(y, k, Y), z),
        )

    for k in range(1, Y):
        nb_copy(k, y).start()
    for k in range(1, REP):
        feature_copy(k, turn(rep, k, REP), rep).start()
    later[0].wait()
    pair = in_rep(x * 2 + 1 - core)
    pair_f = remote(lhs.at[mine], lhs.at[mine], ps.at[0], pr.at[0], pair)
    pair_f.start()
    own_rows = pl.ds(pl.multiple_of(rep * 64, 64), 64)
    own_f[own_rows] = zbuf[z * 8 + rep]

    def ring_step(step, carry):
        for piece in range(SUB):
            for way in range(2):
                arriving(way, step - 1, piece).wait_recv()
                sent(way, step, piece).start()
        return carry

    lax.fori_loop(1, 4, ring_step, 0)

    for k in range(1, Y):
        nb_copy(k, turn(y, -k, Y)).wait_recv()
    to_smem = pltpu.make_async_copy(nb_all, nb_s, load_sem.at[13])
    to_smem.start()
    later[1].wait()
    ones = jnp.ones((8, 128), BF)
    for b in range(8):
        total = dot(ones, adj[b, 0], 1, 1) + dot(ones, adj[b, 1], 1, 1)
        scale[b] = 1.0 / jnp.sqrt(1.0 + total)
    to_smem.wait()

    lax.fori_loop(4, 6, ring_step, 0)
    for k in range(1, REP):
        feature_copy(k, rep, turn(rep, -k, REP)).wait_recv()
    later[2].wait()
    pre_self[...] = dot(own_f[...], ws[...], 0, 0)
    lax.fori_loop(6, HALF - 1, ring_step, 0)
    for piece in range(SUB):
        for way in range(2):
            arriving(way, HALF - 2, piece).wait_recv()
            if way == last_way(piece):
                sent(way, HALF - 1, piece).start()
    for piece in range(SUB):
        arriving(last_way(piece), HALF - 1, piece).wait_recv()

    def wanted(yy, u):
        return nb_s[yy, u // 8, u % 8]

    def far_copy(way):
        return remote(
            far_out.at[way], far_in.at[way], fs.at[7 + way], fr.at[7 + way],
            in_rows(y_next if way == 0 else y_prev, z),
        )

    def near_copy(way, k):
        at = pl.ds(8 * k, 8)
        return remote(
            near_out.at[way, at], near_in.at[way, at], ys.at[way, k], yr.at[way, k],
            in_rows(y_next if way == 0 else y_prev, z),
        )

    for way in range(2):
        for i in range(8):
            far_out[way, i] = zbuf[lax.rem(wanted(y_far, 8 * way + i), 128)]
        far_copy(way).start()
    for way in range(2):
        k = 1 - way
        for i in range(8):
            u = 8 * k + i
            near_out[way, u] = zbuf[lax.rem(wanted(y_next if way == 0 else y_prev, u), 128)]
        near_copy(way, k).start()
    for way in range(2):
        far_copy(way).wait_recv()
        for i in range(8):
            u = 8 * way + i
            block = wanted(y_next if way == 0 else y_prev, u)
            here = block // 128 == y
            near_out[way, u] = jnp.where(here, zbuf[lax.rem(block, 128)], far_in[way, i])
        near_copy(way, way).start()

    for way in range(2):
        near_copy(way, 1 - way).wait_recv()
    for way in range(2):
        near_copy(way, way).wait_recv()

    def use(u):
        block = wanted(y, u)
        ahead = lax.rem(block // 128 - y + Y, Y)
        if u < 8:
            way = jnp.where(ahead == 1, 1, 0)
        else:
            way = jnp.where(ahead == Y - 1, 0, 1)
        return jnp.where(ahead == 0, zbuf[lax.rem(block, 128)], near_in[way, u])

    def agg_copy(k, q, source):
        return remote(
            lhs.at[mine_a, pl.ds(pl.multiple_of(q * 128, 128), 128)],
            own_a.at[pl.ds(pl.multiple_of(source * 64, 64), 64)],
            as_.at[k - 1], ar.at[k - 1], in_rep(q),
        )

    for b in range(8):
        raw = dot(use(b), adj[b, 0], 1, 1) + dot(use(8 + b), adj[b, 1], 1, 1)
        agg = (raw * scale[b, 0:1, :]).astype(BF)
        lhs[mine_a, pl.ds(128 * b, 128)] = agg
    for k in range(1, REP):
        agg_copy(k, turn(rep, k, REP), rep).start()
    pair_a = remote(lhs.at[mine_a], lhs.at[mine_a], ps.at[1], pr.at[1], pair)
    pair_a.start()
    own_a[own_rows] = lhs[mine_a, pl.ds(pl.multiple_of(rep * 128, 128), 128)]
    later[3].wait()
    later[4].wait()
    for k in range(1, REP):
        agg_copy(k, rep, turn(rep, -k, REP)).wait_recv()

    pre = pre_self[...] + dot(own_a[...], wn[...], 0, 0)
    s = 1.0 / (1.0 + jnp.exp(-pre))
    out_ref[...] = (pre * s).astype(BF)
    g_own[...] = (cot[...].astype(F32) * (s * (1.0 + pre * (1.0 - s)))).astype(BF)

    def g_copy(k, q, source):
        return remote(
            g_own.at[:, pl.ds(pl.multiple_of(lax.rem(q, 2) * 256, 256), 256)],
            g_all.at[pl.ds(pl.multiple_of(source * 128, 128), 128)],
            gs.at[k - 1], gr.at[k - 1], in_rep(q),
        )

    for k in (4, 3, 5, 2, 6, 1, 7):
        g_copy(k, turn(rep, k, REP), rep).start()
    g_all[pl.ds(pl.multiple_of(rep * 128, 128), 128)] = g_own[
        :, pl.ds(pl.multiple_of(core * 256, 256), 256)
    ]
    other = pl.ds(pl.multiple_of(64 - core * 64, 64), 64)
    other_a = pl.ds(pl.multiple_of(192 - core * 64, 64), 64)
    remote(lhs.at[other], lhs.at[other], ps.at[0], pr.at[0], pair).wait_recv()
    remote(lhs.at[other_a], lhs.at[other_a], ps.at[1], pr.at[1], pair).wait_recv()
    for k in range(1, REP):
        g_copy(k, rep, turn(rep, -k, REP)).wait_recv()
    grad = dot(lhs[...], g_all[...], 1, 0)
    for q in range(4):
        cols = slice(64 * q, 64 * q + 64)
        parts[q] = jnp.concatenate([grad[:128, cols], grad[128:, cols]], axis=1)

    def part_copy(k, source):
        yy = turn(y, k, Y)
        return remote(
            parts.at[yy], y_in.at[source], ts.at[k - 1], tr.at[k - 1], in_rows(yy, z)
        )

    for k in (2, 1, 3):
        part_copy(k, y).start()
    total = parts[y]
    for k in range(1, Y):
        source = turn(y, -k, Y)
        part_copy(k, source).wait_recv()
        total = total + y_in[source]
    y_sum[...] = total.reshape(Z, 8, 128)

    def is_self(a):
        return jnp.logical_and(x * Z + a == row, 4 * core + y == rep)

    def last_copy(a, source):
        return remote(
            y_sum.at[a], z_in.at[source], us.at[a], ur.at[source],
            {"rows": x * Z + a, "rep": 4 * core + y},
        )

    def send_last(a, carry):
        @pl.when(is_self(a))
        def _():
            pltpu.make_async_copy(y_sum.at[a], z_in.at[z], ur.at[z]).start()

        @pl.when(jnp.logical_not(is_self(a)))
        def _():
            last_copy(a, z).start()

        return carry

    lax.fori_loop(0, Z, send_last, 0)

    for c in [pair_f, pair_a]:
        c.wait_send()
    for k in range(1, REP):
        feature_copy(k, turn(rep, k, REP), rep).wait_send()
        agg_copy(k, turn(rep, k, REP), rep).wait_send()
        g_copy(k, turn(rep, k, REP), rep).wait_send()
    for k in range(1, Y):
        nb_copy(k, y).wait_send()
        part_copy(k, y).wait_send()
    for way in range(2):
        far_copy(way).wait_send()
        for k in range(2):
            near_copy(way, k).wait_send()

    def ring_left(step, carry):
        for piece in range(SUB):
            for way in range(2):
                sent(way, step, piece).wait_send()
        return carry

    lax.fori_loop(0, HALF - 1, ring_left, 0)
    for piece in range(SUB):
        sent(last_way(piece), HALF - 1, piece).wait_send()

    def wait_last(a, carry):
        @pl.when(jnp.logical_not(is_self(a)))
        def _():
            last_copy(a, z).wait_send()

        last_copy(a, a).wait_recv()
        return carry

    lax.fori_loop(0, Z, wait_last, 0)
    grads = z_in[0]
    for a in range(1, Z):
        grads = grads + z_in[a]
    wg_ref[0] = grads[:, :64]
    wg_ref[1] = grads[:, 64:]


def local(features, neighbor_blocks, adjacency, w_self, w_neigh, cotangent):
    vmem, anywhere = pl.BlockSpec(memory_space=pltpu.VMEM), pl.BlockSpec(memory_space=pl.ANY)
    dma = pltpu.SemaphoreType.DMA
    return pl.pallas_call(
        kernel,
        out_shape=(
            jax.ShapeDtypeStruct((128, 512), BF),
            jax.ShapeDtypeStruct((2, 8, 64), F32),
        ),
        in_specs=[vmem] + [anywhere] * 5,
        out_specs=(vmem, vmem),
        scratch_shapes=[
            pltpu.VMEM((128, 64, 128), BF),
            pltpu.VMEM((2, 8, 64, 128), BF),
            pltpu.VMEM((2, 8, 64, 128), BF),
            pltpu.VMEM((2, 16, 64, 128), BF),
            pltpu.VMEM((2, 16, 64, 128), BF),
            pltpu.VMEM((512, 128), BF),
            pltpu.VMEM((512, 128), BF),
            pltpu.VMEM((256, 1024), BF),
            pltpu.VMEM((8, 2, 128, 128), BF),
            pltpu.VMEM((512, 512), BF),
            pltpu.VMEM((512, 512), BF),
            pltpu.VMEM((128, 512), BF),
            pltpu.VMEM((8, 8, 128), F32),
            pltpu.VMEM((128, 512), F32),
            pltpu.VMEM((128, 512), BF),
            pltpu.VMEM((1024, 256), BF),
            pltpu.VMEM((4, 128, 128), F32),
            pltpu.VMEM((4, 128, 128), F32),
            pltpu.VMEM((16, 8, 128), F32),
            pltpu.VMEM((16, 8, 128), F32),
            pltpu.VMEM((4, 2, 8), jnp.int32),
            pltpu.SMEM((4, 2, 8), jnp.int32),
            dma((14,)),
            dma((2, HALF, SUB)), dma((2, HALF, SUB)),
            dma((9,)), dma((9,)),
            dma((7,)), dma((7,)),
            dma((7,)), dma((7,)),
            dma((2,)), dma((2,)),
            dma((3,)), dma((3,)),
            dma((2, 2)), dma((2, 2)),
            dma((3,)), dma((3,)),
            dma((16,)), dma((16,)),
        ],
        compiler_params=pltpu.CompilerParams(
            collective_id=0, has_side_effects=True, vmem_limit_bytes=32 * 1024 * 1024
        ),
        cost_estimate=pl.CostEstimate(
            flops=500_000_000, bytes_accessed=2_500_000, transcendentals=65536
        ),
    )(neighbor_blocks.T, features.T, adjacency, w_self, w_neigh, cotangent)


def solution(mesh):
    in_specs = (
        P("rows", "rep"),
        P("rows", None),
        P("rows", None, None, None),
        P(),
        P(),
        P(("rows", "rep"), None),
    )
    out_specs = (P(("rows", "rep"), None), P(None, "rows", "rep"))
    return jax.shard_map(local, mesh=mesh, in_specs=in_specs, out_specs=out_specs, check_vma=False)
```

time: 488 us -> 88 us (0.18)
  the two profiles are of different devices: /device:TPU:6 before, /device:TPU:16 now
where the time goes in v1:
time: 88 us; the launch traced here: 87.7 us
  Pallas kernels  80.2 us (91%)
  local copies, waits for them, and re-layouts  6.86 us (8%)
    pallas_call x1, Pallas kernels, local(): pl.pallas_call(kernel, out_shape=(jax.ShapeDtypeStruct((128, 512), BF), j...  80.2 us
    unnamed x14, local copies, waits for them, and re-layouts  6.86 us

profile of v1, /device:TPU:16, one launch (start us, length us, event | category | flops | bytes accessed | tf_op | source)
XLA Modules:
  0.0 87.7 jit_solution(8383896254517605337)
XLA Ops:
  0.6 0.0 copy-start.5
  0.6 0.7 copy-done.5
  1.3 0.0 copy-start
  1.3 1.0 %copy-done = bf16[8,2,128,128]{3,2,1,0:T(8,128)(2,1)S(1)} copy-done((bf16[8,2,128,128]{3,2,1,0:T(8,128)(2,1)S(1)}, bf16[8,2,128,128]{3,2,1,0:T(8,128)(2,1)}, u32[]{:S(2)}) %copy-start) | copy-done | bytes 524312
  2.4 0.0 copy-start.1
  2.4 1.0 %copy-done.1 = bf16[512,512]{1,0:T(8,128)(2,1)S(1)} copy-done((bf16[512,512]{1,0:T(8,128)(2,1)S(1)}, bf16[512,512]{1,0:T(8,128)(2,1)}, u32[]{:S(2)}) %copy-start.1) | copy-done | bytes 524312
  3.4 0.0 copy-start.2
  3.4 1.0 %copy-done.2 = bf16[512,512]{1,0:T(8,128)(2,1)S(1)} copy-done((bf16[512,512]{1,0:T(8,128)(2,1)S(1)}, bf16[512,512]{1,0:T(8,128)(2,1)}, u32[]{:S(2)}) %copy-start.2) | copy-done | bytes 524312
  4.4 0.0 copy-start.3
  4.4 0.9 %copy-done.3 = bf16[1024,64]{0,1:T(8,128)(2,1)S(1)} copy-done((bf16[1024,64]{0,1:T(8,128)(2,1)S(1)}, bf16[1024,64]{0,1:T(8,128)(2,1)}, u32[]{:S(2)}) %copy-start.3) | copy-done | bytes 131096
  5.3 0.0 copy-start.4
  5.3 0.9 %copy-done.4 = bf16[128,512]{1,0:T(8,128)(2,1)S(1)} copy-done((bf16[128,512]{1,0:T(8,128)(2,1)S(1)}, bf16[128,512]{1,0:T(8,128)(2,1)}, u32[]{:S(2)}) %copy-start.4) | copy-done | bytes 131096
  6.2 80.2 %shard_map.77 = (bf16[128,512]{1,0:T(8,128)(2,1)S(1)}, f32[2,8,64]{2,1,0:T(8,128)S(1)}) custom-call(s32[2,8]{1,0:T(2,128)S(1)} %bitcast.3, bf16[64,1024]{1,0:T(8,128)(2,1)S(1)} %bitcast.2, bf16[8,2,128,128]{3,2,1,0:T(8,128)(2,1)S(1)} %copy-done, bf16[512,512]{1,0:T(8,128)(2,1)S(1)} %copy-done.1, bf16[512,512]{1,0:T(8,128)(2,1)S(1)} %copy-done.2, ...), custom_call_target="tpu_custom_call" | custom-call | flops 500000000 | bytes 2500000 | tf_op jit(solution)/shard_map/pallas_call | solution.py:339
  86.5 0.7 copy.10
  87.1 0.6 copy.11
Async XLA Ops:
  0.6 0.7 copy-start.5
  1.3 1.0 %copy-start = (bf16[8,2,128,128]{3,2,1,0:T(8,128)(2,1)S(1)}, bf16[8,2,128,128]{3,2,1,0:T(8,128)(2,1)}, u32[]{:S(2)}) copy-start(bf16[8,2,128,128]{3,2,1,0:T(8,128)(2,1)} %adj_hbm.1) | copy-start | bytes 1572868
  2.4 1.0 %copy-start.1 = (bf16[512,512]{1,0:T(8,128)(2,1)S(1)}, bf16[512,512]{1,0:T(8,128)(2,1)}, u32[]{:S(2)}) copy-start(bf16[512,512]{1,0:T(8,128)(2,1)} %ws_hbm.1) | copy-start | bytes 1572868
  3.4 1.0 %copy-start.2 = (bf16[512,512]{1,0:T(8,128)(2,1)S(1)}, bf16[512,512]{1,0:T(8,128)(2,1)}, u32[]{:S(2)}) copy-start(bf16[512,512]{1,0:T(8,128)(2,1)} %wn_hbm.1) | copy-start | bytes 1572868
  4.4 0.9 %copy-start.3 = (bf16[1024,64]{0,1:T(8,128)(2,1)S(1)}, bf16[1024,64]{0,1:T(8,128)(2,1)}, u32[]{:S(2)}) copy-start(bf16[1024,64]{0,1:T(8,128)(2,1)} %param.6) | copy-start | bytes 393220
  5.3 0.9 %copy-start.4 = (bf16[128,512]{1,0:T(8,128)(2,1)S(1)}, bf16[128,512]{1,0:T(8,128)(2,1)}, u32[]{:S(2)}) copy-start(bf16[128,512]{1,0:T(8,128)(2,1)} %cot_hbm.1) | copy-start | bytes 393220

commit v2 on v1

v2 whole, which is shorter than its diff:
```python
import jax
import jax.numpy as jnp
from jax import lax
from jax.experimental import pallas as pl
from jax.experimental.pallas import tpu as pltpu
from jax.sharding import PartitionSpec as P

Y, Z, X = 4, 16, 4
REP = 2 * X
SUB = 4
PIECE = 8 // SUB
HALF = Z // 2
MESH = pl.DeviceIdType.MESH
BF, F32 = jnp.bfloat16, jnp.float32


def dot(a, b, ca, cb):
    return lax.dot_general(a, b, (((ca,), (cb,)), ((), ())), preferred_element_type=F32)


def kernel(
    nb_ref, f_hbm, adj_hbm, ws_hbm, wn_hbm, cot_hbm,
    out_ref, wg_ref,
    zbuf, hold, picked, used, own_f, own_a, lhs, adj, ws, wn, cot,
    scale, pre_self, g_own, g_all, parts, y_in, y_sum, z_in, table, asked, nb_s, table_s, asked_s,
    load_sem, zs, zr, fs, fr, as_, ar, gs, gr, ps, pr, ns, nr, ys, yr, ts, tr, us, ur,
):
    row, rep = lax.axis_index("rows"), lax.axis_index("rep")
    y, z = row // Z, lax.rem(row, Z)
    x, core = rep // 2, lax.rem(rep, 2)

    def in_rows(yy, zz):
        return {"rows": yy * Z + zz, "rep": rep}

    def in_rep(q):
        return {"rows": row, "rep": q}

    def remote(src, dst, send, recv, device):
        return pltpu.make_async_remote_copy(
            src_ref=src, dst_ref=dst, send_sem=send, recv_sem=recv,
            device_id=device, device_id_type=MESH,
        )

    def turn(a, k, n):
        return lax.rem(a + k + n, n)

    right, left = in_rows(y, turn(z, 1, Z)), in_rows(y, turn(z, -1, Z))

    ends = []

    def go(copy):
        copy.start()
        ends.append(copy.wait_send)

    def finish():
        for end in ends:
            end()
        ends.clear()

    first = [
        pltpu.make_async_copy(
            f_hbm.at[:, pl.ds(128 * l, 128)], zbuf.at[z * 8 + l], load_sem.at[l]
        )
        for l in range(8)
    ]
    mine = pl.ds(pl.multiple_of(core * 64, 64), 64)
    mine_a = pl.ds(pl.multiple_of(128 + core * 64, 64), 64)
    later = [
        pltpu.make_async_copy(f_hbm, lhs.at[mine], load_sem.at[8]),
        pltpu.make_async_copy(adj_hbm, adj, load_sem.at[9]),
        pltpu.make_async_copy(ws_hbm, ws, load_sem.at[10]),
        pltpu.make_async_copy(wn_hbm, wn, load_sem.at[11]),
        pltpu.make_async_copy(cot_hbm, cot, load_sem.at[12]),
    ]
    for c in first + later:
        c.start()

    barrier = pltpu.get_barrier_semaphore()
    for device in (right, left):
        pl.semaphore_signal(barrier, inc=1, device_id=device, device_id_type=MESH)
    for k in range(1, Y):
        pl.semaphore_signal(
            barrier, inc=1, device_id=in_rows(turn(y, k, Y), z), device_id_type=MESH
        )
    for k in range(1, REP):
        pl.semaphore_signal(
            barrier, inc=1, device_id=in_rep(turn(rep, k, REP)), device_id_type=MESH
        )
    owner_id = lax.broadcasted_iota(jnp.int32, (64, 8), 0)
    lane = lax.broadcasted_iota(jnp.int32, (64, 8), 1)
    low = jnp.full((64, 1), 255, jnp.int32)
    high = jnp.zeros((64, 1), jnp.int32)
    for k in range(2):
        block = nb_ref[k : k + 1, :]
        named = block // 8 == owner_id
        code = (8 * k + lane) * 8 + block % 8
        low = jnp.minimum(low, jnp.min(jnp.where(named, code, 255), axis=1, keepdims=True))
        high = jnp.maximum(high, jnp.max(jnp.where(named, code, 0), axis=1, keepdims=True))
    lane = lax.broadcasted_iota(jnp.int32, (64, 128), 1)
    table[...] = jnp.where(lane == 0, low % 8, jnp.where(lane == 1, high % 8, low // 8))
    to_smem = [
        pltpu.make_async_copy(nb_ref, nb_s, load_sem.at[13]),
        pltpu.make_async_copy(table, table_s, load_sem.at[14]),
    ]
    for c in to_smem:
        c.start()
    for c in first:
        c.wait()
    pl.semaphore_wait(barrier, 2 + (Y - 1) + (REP - 1))

    def table_copy(k):
        yy = turn(y, k, Y)
        return remote(
            table.at[pl.ds(yy * Z, Z)], asked.at[Y - k - 1], ns.at[k - 1], nr.at[k - 1],
            in_rows(yy, z),
        )

    for k in (2, 1, 3):
        go(table_copy(k))

    def ring_copy(way, step, piece, chunk):
        at = pl.ds(chunk * 8 + piece * PIECE, PIECE)
        return remote(
            zbuf.at[at], zbuf.at[at], zs.at[way, step, piece], zr.at[way, step, piece],
            right if way == 0 else left,
        )

    def sent(way, step, piece):
        return ring_copy(way, step, piece, turn(z, -step if way == 0 else step, Z))

    def arriving(way, step, piece):
        return ring_copy(way, step, piece, turn(z, -1 - step if way == 0 else 1 + step, Z))

    def last_way(piece):
        return 0 if piece < SUB // 2 else 1

    for piece in range(SUB):
        for way in range(2):
            sent(way, 0, piece).start()

    def feature_copy(k, q, source):
        return remote(
            zbuf.at[z * 8 + q], own_f.at[pl.ds(pl.multiple_of(source * 64, 64), 64)],
            fs.at[k - 1], fr.at[k - 1], in_rep(q),
        )

    for k in range(1, REP):
        go(feature_copy(k, turn(rep, k, REP), rep))
    later[0].wait()
    pair = in_rep(x * 2 + 1 - core)
    pair_f = remote(lhs.at[mine], lhs.at[mine], ps.at[0], pr.at[0], pair)
    go(pair_f)
    own_rows = pl.ds(pl.multiple_of(rep * 64, 64), 64)
    own_f[own_rows] = zbuf[z * 8 + rep]

    for k in range(1, Y):
        table_copy(k).wait_recv()
    ask_smem = pltpu.make_async_copy(asked, asked_s, load_sem.at[15])
    ask_smem.start()

    def use_copy(k, chunk):
        return remote(
            picked.at[k - 1, chunk], used.at[Y - k - 1, chunk],
            ys.at[k - 1, chunk], yr.at[Y - k - 1, chunk], in_rows(turn(y, k, Y), z),
        )

    def send_uses(chunk):
        hold[...] = zbuf[pl.ds(chunk * 8, 8)]
        for k in (2, 1, 3):
            for rank in range(2):
                picked[k - 1, chunk, rank] = hold[asked_s[k - 1, chunk, rank]]
            use_copy(k, chunk).start()

    ask_smem.wait()
    send_uses(z)

    def ring_step(step, carry):
        for piece in range(SUB):
            for way in range(2):
                arriving(way, step - 1, piece).wait_recv()
                sent(way, step, piece).start()
        for way in range(2):
            send_uses(turn(z, -step if way == 0 else step, Z))
        return carry

    lax.fori_loop(1, HALF - 1, ring_step, 0)
    for piece in range(SUB):
        for way in range(2):
            arriving(way, HALF - 2, piece).wait_recv()
            if way == last_way(piece):
                sent(way, HALF - 1, piece).start()
    for way in range(2):
        send_uses(turn(z, 1 - HALF if way == 0 else HALF - 1, Z))
    for piece in range(SUB):
        arriving(last_way(piece), HALF - 1, piece).wait_recv()
    send_uses(turn(z, HALF, Z))

    def ring_left(step, carry):
        for piece in range(SUB):
            for way in range(2):
                sent(way, step, piece).wait_send()
        return carry

    def ring_end():
        lax.fori_loop(0, HALF - 1, ring_left, 0)
        for piece in range(SUB):
            sent(last_way(piece), HALF - 1, piece).wait_send()

    ends.append(ring_end)

    def used_here(chunk, carry):
        for k in range(1, Y):
            use_copy(k, chunk).wait_recv()
        return carry

    def uses_left(chunk, carry):
        for k in range(1, Y):
            use_copy(k, chunk).wait_send()
        return carry

    ends.append(lambda: lax.fori_loop(0, Z, uses_left, 0))
    later[1].wait()
    ones = jnp.ones((8, 128), BF)
    for b in range(8):
        total = dot(ones, adj[b, 0], 1, 1) + dot(ones, adj[b, 1], 1, 1)
        scale[b] = 1.0 / jnp.sqrt(1.0 + total)
    for c in to_smem:
        c.wait()
    for k in range(1, REP):
        feature_copy(k, rep, turn(rep, -k, REP)).wait_recv()
    later[2].wait()
    pre_self[...] = dot(own_f[...], ws[...], 0, 0)
    lax.fori_loop(0, Z, used_here, 0)
    def use(u):
        block = nb_s[u // 8, u % 8]
        owner = block // 8
        ahead = lax.rem(owner // Z - y + Y, Y)
        rank = jnp.where(table_s[owner, 2] == u, 0, 1)
        other = used[jnp.maximum(ahead, 1) - 1, lax.rem(owner, Z), rank]
        return jnp.where(ahead == 0, zbuf[lax.rem(block, 8 * Z)], other)

    def agg_copy(k, q, source):
        return remote(
            lhs.at[mine_a, pl.ds(pl.multiple_of(q * 128, 128), 128)],
            own_a.at[pl.ds(pl.multiple_of(source * 64, 64), 64)],
            as_.at[k - 1], ar.at[k - 1], in_rep(q),
        )

    for b in range(8):
        raw = dot(use(b), adj[b, 0], 1, 1) + dot(use(8 + b), adj[b, 1], 1, 1)
        agg = (raw * scale[b, 0:1, :]).astype(BF)
        lhs[mine_a, pl.ds(128 * b, 128)] = agg
    for k in range(1, REP):
        go(agg_copy(k, turn(rep, k, REP), rep))
    pair_a = remote(lhs.at[mine_a], lhs.at[mine_a], ps.at[1], pr.at[1], pair)
    go(pair_a)
    finish()
    own_a[own_rows] = lhs[mine_a, pl.ds(pl.multiple_of(rep * 128, 128), 128)]
    later[3].wait()
    later[4].wait()
    for k in range(1, REP):
        agg_copy(k, rep, turn(rep, -k, REP)).wait_recv()

    pre = pre_self[...] + dot(own_a[...], wn[...], 0, 0)
    s = 1.0 / (1.0 + jnp.exp(-pre))
    out_ref[...] = (pre * s).astype(BF)
    g_own[...] = (cot[...].astype(F32) * (s * (1.0 + pre * (1.0 - s)))).astype(BF)


    def g_copy(k, q, source):
        return remote(
            g_own.at[:, pl.ds(pl.multiple_of(lax.rem(q, 2) * 256, 256), 256)],
            g_all.at[pl.ds(pl.multiple_of(source * 128, 128), 128)],
            gs.at[k - 1], gr.at[k - 1], in_rep(q),
        )

    for k in (4, 3, 5, 2, 6, 1, 7):
        go(g_copy(k, turn(rep, k, REP), rep))
    g_all[pl.ds(pl.multiple_of(rep * 128, 128), 128)] = g_own[
        :, pl.ds(pl.multiple_of(core * 256, 256), 256)
    ]
    finish()
    other = pl.ds(pl.multiple_of(64 - core * 64, 64), 64)
    other_a = pl.ds(pl.multiple_of(192 - core * 64, 64), 64)
    remote(lhs.at[other], lhs.at[other], ps.at[0], pr.at[0], pair).wait_recv()
    remote(lhs.at[other_a], lhs.at[other_a], ps.at[1], pr.at[1], pair).wait_recv()
    for k in range(1, REP):
        g_copy(k, rep, turn(rep, -k, REP)).wait_recv()
    grad = dot(lhs[...], g_all[...], 1, 0)
    for q in range(4):
        cols = slice(64 * q, 64 * q + 64)
        parts[q] = jnp.concatenate([grad[:128, cols], grad[128:, cols]], axis=1)

    def part_copy(k, source):
        yy = turn(y, k, Y)
        return remote(
            parts.at[yy], y_in.at[source], ts.at[k - 1], tr.at[k - 1], in_rows(yy, z)
        )

    for k in (2, 1, 3):
        go(part_copy(k, y))
    total = parts[y]
    for k in range(1, Y):
        source = turn(y, -k, Y)
        part_copy(k, source).wait_recv()
        total = total + y_in[source]
    y_sum[...] = total.reshape(Z, 8, 128)

    def last_copy(j, source):
        a = turn(z, j, Z)
        return remote(
            y_sum.at[a], z_in.at[source], us.at[j], ur.at[j],
            {"rows": x * Z + a, "rep": 4 * core + y},
        )

    kept = jnp.logical_and(x == y, 4 * core + y == rep)
    keep = pltpu.make_async_copy(y_sum.at[z], z_in.at[z], ur.at[0])
    for j in (8, 7, 9, 6, 10, 5, 11, 4, 12, 3, 13, 2, 14, 1, 15):
        last_copy(j, z).start()

    @pl.when(kept)
    def _():
        keep.start()

    @pl.when(jnp.logical_not(kept))
    def _():
        last_copy(0, z).start()

    finish()
    for j in range(Z):
        last_copy(j, turn(z, -j, Z)).wait_recv()
    grads = z_in[0]
    for a in range(1, Z):
        grads = grads + z_in[a]
    wg_ref[0] = grads[:, :64]
    wg_ref[1] = grads[:, 64:]
    for j in range(1, Z):
        last_copy(j, z).wait_send()

    @pl.when(jnp.logical_not(kept))
    def _():
        last_copy(0, z).wait_send()


def local(features, neighbor_blocks, adjacency, w_self, w_neigh, cotangent):
    vmem, anywhere = pl.BlockSpec(memory_space=pltpu.VMEM), pl.BlockSpec(memory_space=pl.ANY)
    dma = pltpu.SemaphoreType.DMA
    return pl.pallas_call(
        kernel,
        out_shape=(
            jax.ShapeDtypeStruct((128, 512), BF),
            jax.ShapeDtypeStruct((2, 8, 64), F32),
        ),
        in_specs=[vmem] + [anywhere] * 5,
        out_specs=(vmem, vmem),
        scratch_shapes=[
            pltpu.VMEM((128, 64, 128), BF),
            pltpu.VMEM((8, 64, 128), BF),
            pltpu.VMEM((3, 16, 2, 64, 128), BF),
            pltpu.VMEM((3, 16, 2, 64, 128), BF),
            pltpu.VMEM((512, 128), BF),
            pltpu.VMEM((512, 128), BF),
            pltpu.VMEM((256, 1024), BF),
            pltpu.VMEM((8, 2, 128, 128), BF),
            pltpu.VMEM((512, 512), BF),
            pltpu.VMEM((512, 512), BF),
            pltpu.VMEM((128, 512), BF),
            pltpu.VMEM((8, 8, 128), F32),
            pltpu.VMEM((128, 512), F32),
            pltpu.VMEM((128, 512), BF),
            pltpu.VMEM((1024, 256), BF),
            pltpu.VMEM((4, 128, 128), F32),
            pltpu.VMEM((4, 128, 128), F32),
            pltpu.VMEM((16, 8, 128), F32),
            pltpu.VMEM((16, 8, 128), F32),
            pltpu.VMEM((64, 128), jnp.int32),
            pltpu.VMEM((3, 16, 128), jnp.int32),
            pltpu.SMEM((2, 8), jnp.int32),
            pltpu.SMEM((64, 128), jnp.int32),
            pltpu.SMEM((3, 16, 128), jnp.int32),
            dma((16,)),
            dma((2, HALF, SUB)), dma((2, HALF, SUB)),
            dma((7,)), dma((7,)),
            dma((7,)), dma((7,)),
            dma((7,)), dma((7,)),
            dma((2,)), dma((2,)),
            dma((3,)), dma((3,)),
            dma((3, 16)), dma((3, 16)),
            dma((3,)), dma((3,)),
            dma((16,)), dma((16,)),
        ],
        compiler_params=pltpu.CompilerParams(
            collective_id=0, has_side_effects=True, vmem_limit_bytes=60 * 1024 * 1024
        ),
        cost_estimate=pl.CostEstimate(
            flops=500_000_000, bytes_accessed=2_500_000, transcendentals=65536
        ),
    )(neighbor_blocks.T, features.T, adjacency, w_self, w_neigh, cotangent)


def solution(mesh):
    in_specs = (
        P("rows", "rep"),
        P("rows", None),
        P("rows", None, None, None),
        P(),
        P(),
        P(("rows", "rep"), None),
    )
    out_specs = (P(("rows", "rep"), None), P(None, "rows", "rep"))
    return jax.shard_map(local, mesh=mesh, in_specs=in_specs, out_specs=out_specs, check_vma=False)
```

time: 88 us -> 80.6 us (0.916)
  local copies, waits for them, and re-layouts: 6.86 us -> 2.18 us
  Pallas kernels: 80.2 us -> 77.6 us
    unnamed x14 -> x4, local copies, waits for them, and re-layouts: 6.86 us -> 2.18 us
    pallas_call x1, Pallas kernels: 80.2 us -> 77.6 us  [local(): pl.pallas_call(kernel, out_shape=(jax.ShapeDtypeStruct((128, 512), BF), j...]
where the time goes in v2:
time: 80.6 us; the launch traced here: 80.4 us
  Pallas kernels  77.6 us (96%)
  local copies, waits for them, and re-layouts  2.18 us (3%)
    pallas_call x1, Pallas kernels, local(): pl.pallas_call(kernel, out_shape=(jax.ShapeDtypeStruct((128, 512), BF), j...  77.6 us
    unnamed x4, local copies, waits for them, and re-layouts  2.18 us

profile of v2, /device:TPU:16, one launch (start us, length us, event | category | flops | bytes accessed | tf_op | source)
XLA Modules:
  0.0 80.4 jit_solution(17478738842507494068)
XLA Ops:
  0.6 77.6 %shard_map.77 = (bf16[128,512]{1,0:T(8,128)(2,1)}, f32[2,8,64]{2,1,0:T(8,128)}) custom-call(s32[2,8]{1,0:T(2,128)} %bitcast.3, bf16[64,1024]{1,0:T(8,128)(2,1)} %bitcast.2, bf16[8,2,128,128]{3,2,1,0:T(8,128)(2,1)} %adj_hbm.1, bf16[512,512]{1,0:T(8,128)(2,1)} %ws_hbm.1, bf16[512,512]{1,0:T(8,128)(2,1)} %wn_hbm.1, bf16[128,512]{1,0:T(8,128)(2,1)} %cot_hbm.1), custom_call_target="tpu_custom_call" | custom-call | flops 500000000 | bytes 2500000 | tf_op jit(solution)/shard_map/pallas_call | solution.py:348
  78.2 0.0 copy-start
  78.2 1.6 %copy.10 = bf16[128,512]{1,0:T(8,128)(2,1)} copy(bf16[128,512]{1,0:T(8,128)(2,1)} %get-tuple-element.4) | data formatting | bytes 262144
  79.8 0.0 copy-done
  79.8 0.6 copy.11
Async XLA Ops:
  78.2 1.6 %copy-start = (f32[2,8,64]{2,1,0:T(8,128)S(1)}, f32[2,8,64]{2,1,0:T(8,128)}, u32[]{:S(2)}) copy-start(f32[2,8,64]{2,1,0:T(8,128)} %get-tuple-element.5) | copy-start | bytes 12292

commit v3 on v2

--- a/solution.py
+++ b/solution.py
@@ -121,7 +121,7 @@
     def ring_copy(way, step, piece, chunk):
         at = pl.ds(chunk * 8 + piece * PIECE, PIECE)
         return remote(
-            zbuf.at[at], zbuf.at[at], zs.at[way, step, piece], zr.at[way, step, piece],
+            zbuf.at[at], zbuf.at[at], zs.at[way], zr.at[way, step, piece],
             right if way == 0 else left,
         )
 
@@ -141,11 +141,14 @@
     def feature_copy(k, q, source):
         return remote(
             zbuf.at[z * 8 + q], own_f.at[pl.ds(pl.multiple_of(source * 64, 64), 64)],
-            fs.at[k - 1], fr.at[k - 1], in_rep(q),
+            fs.at[0], fr.at[0], in_rep(q),
         )
 
     for k in range(1, REP):
-        go(feature_copy(k, turn(rep, k, REP), rep))
+        feature_copy(k, turn(rep, k, REP), rep).start()
+    some_f = own_f.at[pl.ds(0, 448)]
+    all_f = remote(some_f, some_f, fs.at[0], fr.at[0], in_rep(turn(rep, 1, REP)))
+    ends.append(all_f.wait_send)
     later[0].wait()
     pair = in_rep(x * 2 + 1 - core)
     pair_f = remote(lhs.at[mine], lhs.at[mine], ps.at[0], pr.at[0], pair)
@@ -161,7 +164,7 @@
     def use_copy(k, chunk):
         return remote(
             picked.at[k - 1, chunk], used.at[Y - k - 1, chunk],
-            ys.at[k - 1, chunk], yr.at[Y - k - 1, chunk], in_rows(turn(y, k, Y), z),
+            ys.at[k - 1], yr.at[Y - k - 1], in_rows(turn(y, k, Y), z),
         )
 
     def send_uses(chunk):
@@ -195,30 +198,24 @@
         arriving(last_way(piece), HALF - 1, piece).wait_recv()
     send_uses(turn(z, HALF, Z))
 
-    def ring_left(step, carry):
-        for piece in range(SUB):
-            for way in range(2):
-                sent(way, step, piece).wait_send()
-        return carry
-
     def ring_end():
-        lax.fori_loop(0, HALF - 1, ring_left, 0)
-        for piece in range(SUB):
-            sent(last_way(piece), HALF - 1, piece).wait_send()
+        for way in range(2):
+            all_sent = zbuf.at[pl.ds(0, 8 * HALF - 4)]
+            remote(all_sent, all_sent, zs.at[way], zr.at[way, 0, 0], right).wait_send()
 
     ends.append(ring_end)
 
-    def used_here(chunk, carry):
+    def all_uses(k):
+        return remote(
+            picked.at[k - 1], used.at[Y - k - 1], ys.at[k - 1], yr.at[Y - k - 1],
+            in_rows(turn(y, k, Y), z),
+        )
+
+    def uses_left():
         for k in range(1, Y):
-            use_copy(k, chunk).wait_recv()
-        return carry
-
-    def uses_left(chunk, carry):
-        for k in range(1, Y):
-            use_copy(k, chunk).wait_send()
-        return carry
-
-    ends.append(lambda: lax.fori_loop(0, Z, uses_left, 0))
+            all_uses(k).wait_send()
+
+    ends.append(uses_left)
     later[1].wait()
     ones = jnp.ones((8, 128), BF)
     for b in range(8):
@@ -226,11 +223,11 @@
         scale[b] = 1.0 / jnp.sqrt(1.0 + total)
     for c in to_smem:
         c.wait()
-    for k in range(1, REP):
-        feature_copy(k, rep, turn(rep, -k, REP)).wait_recv()
+    all_f.wait_recv()
     later[2].wait()
     pre_self[...] = dot(own_f[...], ws[...], 0, 0)
-    lax.fori_loop(0, Z, used_here, 0)
+    for k in range(1, Y):
+        all_uses(k).wait_recv()
     def use(u):
         block = nb_s[u // 8, u % 8]
         owner = block // 8
@@ -243,7 +240,7 @@
         return remote(
             lhs.at[mine_a, pl.ds(pl.multiple_of(q * 128, 128), 128)],
             own_a.at[pl.ds(pl.multiple_of(source * 64, 64), 64)],
-            as_.at[k - 1], ar.at[k - 1], in_rep(q),
+            as_.at[0], ar.at[0], in_rep(q),
         )
 
     for b in range(8):
@@ -251,15 +248,17 @@
         agg = (raw * scale[b, 0:1, :]).astype(BF)
         lhs[mine_a, pl.ds(128 * b, 128)] = agg
     for k in range(1, REP):
-        go(agg_copy(k, turn(rep, k, REP), rep))
+        agg_copy(k, turn(rep, k, REP), rep).start()
+    some_a = own_a.at[pl.ds(0, 448)]
+    all_a = remote(some_a, some_a, as_.at[0], ar.at[0], in_rep(turn(rep, 1, REP)))
     pair_a = remote(lhs.at[mine_a], lhs.at[mine_a], ps.at[1], pr.at[1], pair)
     go(pair_a)
     finish()
     own_a[own_rows] = lhs[mine_a, pl.ds(pl.multiple_of(rep * 128, 128), 128)]
     later[3].wait()
     later[4].wait()
-    for k in range(1, REP):
-        agg_copy(k, rep, turn(rep, -k, REP)).wait_recv()
+    all_a.wait_recv()
+    ends.append(all_a.wait_send)
 
     pre = pre_self[...] + dot(own_a[...], wn[...], 0, 0)
     s = 1.0 / (1.0 + jnp.exp(-pre))
@@ -271,11 +270,13 @@
         return remote(
             g_own.at[:, pl.ds(pl.multiple_of(lax.rem(q, 2) * 256, 256), 256)],
             g_all.at[pl.ds(pl.multiple_of(source * 128, 128), 128)],
-            gs.at[k - 1], gr.at[k - 1], in_rep(q),
+            gs.at[0], gr.at[0], in_rep(q),
         )
 
     for k in (4, 3, 5, 2, 6, 1, 7):
-        go(g_copy(k, turn(rep, k, REP), rep))
+        g_copy(k, turn(rep, k, REP), rep).start()
+    some_g = g_all.at[pl.ds(0, 896)]
+    all_g = remote(some_g, some_g, gs.at[0], gr.at[0], in_rep(turn(rep, 1, REP)))
     g_all[pl.ds(pl.multiple_of(rep * 128, 128), 128)] = g_own[
         :, pl.ds(pl.multiple_of(core * 256, 256), 256)
     ]
@@ -284,62 +285,55 @@
     other_a = pl.ds(pl.multiple_of(192 - core * 64, 64), 64)
     remote(lhs.at[other], lhs.at[other], ps.at[0], pr.at[0], pair).wait_recv()
     remote(lhs.at[other_a], lhs.at[other_a], ps.at[1], pr.at[1], pair).wait_recv()
-    for k in range(1, REP):
-        g_copy(k, rep, turn(rep, -k, REP)).wait_recv()
+    all_g.wait_recv()
+    ends.append(all_g.wait_send)
     grad = dot(lhs[...], g_all[...], 1, 0)
     for q in range(4):
         cols = slice(64 * q, 64 * q + 64)
-        parts[q] = jnp.concatenate([grad[:128, cols], grad[128:, cols]], axis=1)
-
-    def part_copy(k, source):
-        yy = turn(y, k, Y)
-        return remote(
-            parts.at[yy], y_in.at[source], ts.at[k - 1], tr.at[k - 1], in_rows(yy, z)
-        )
-
-    for k in (2, 1, 3):
-        go(part_copy(k, y))
-    total = parts[y]
-    for k in range(1, Y):
-        source = turn(y, -k, Y)
-        part_copy(k, source).wait_recv()
-        total = total + y_in[source]
+        part = jnp.concatenate([grad[:128, cols], grad[128:, cols]], axis=1)
+        parts[q] = part.astype(BF)
+
+    def part_copy(q, source):
+        return remote(
+            parts.at[q], y_in.at[source], ts.at[q], tr.at[source],
+            {"rows": x * Z + z, "rep": 4 * core + q},
+        )
+
+    def part_stays(q):
+        return jnp.logical_and(x == y, 4 * core + q == rep)
+
+    for q in range(4):
+        keep = pltpu.make_async_copy(parts.at[q], y_in.at[y], tr.at[y])
+        stays = part_stays(q)
+        pl.when(stays)(keep.start)
+        pl.when(jnp.logical_not(stays))(part_copy(q, y).start)
+    total = jnp.zeros((128, 128), F32)
+    for source in range(4):
+        part_copy(0, source).wait_recv()
+        total = total + y_in[source].astype(F32)
     y_sum[...] = total.reshape(Z, 8, 128)
 
     def last_copy(j, source):
         a = turn(z, j, Z)
         return remote(
-            y_sum.at[a], z_in.at[source], us.at[j], ur.at[j],
-            {"rows": x * Z + a, "rep": 4 * core + y},
-        )
-
-    kept = jnp.logical_and(x == y, 4 * core + y == rep)
-    keep = pltpu.make_async_copy(y_sum.at[z], z_in.at[z], ur.at[0])
+            y_sum.at[a], z_in.at[source], us.at[0], ur.at[0], in_rows(y, a)
+        )
+
     for j in (8, 7, 9, 6, 10, 5, 11, 4, 12, 3, 13, 2, 14, 1, 15):
         last_copy(j, z).start()
-
-    @pl.when(kept)
-    def _():
-        keep.start()
-
-    @pl.when(jnp.logical_not(kept))
-    def _():
-        last_copy(0, z).start()
-
+    z_in[z] = y_sum[z]
     finish()
-    for j in range(Z):
-        last_copy(j, turn(z, -j, Z)).wait_recv()
+    for q in range(4):
+        pl.when(jnp.logical_not(part_stays(q)))(part_copy(q, y).wait_send)
+    some_z = z_in.at[pl.ds(0, Z - 1)]
+    all_z = remote(some_z, some_z, us.at[0], ur.at[0], right)
+    all_z.wait_recv()
     grads = z_in[0]
     for a in range(1, Z):
         grads = grads + z_in[a]
     wg_ref[0] = grads[:, :64]
     wg_ref[1] = grads[:, 64:]
-    for j in range(1, Z):
-        last_copy(j, z).wait_send()
-
-    @pl.when(jnp.logical_not(kept))
-    def _():
-        last_copy(0, z).wait_send()
+    all_z.wait_send()
 
 
 def local(features, neighbor_blocks, adjacency, w_self, w_neigh, cotangent):
@@ -369,8 +363,8 @@
             pltpu.VMEM((128, 512), F32),
             pltpu.VMEM((128, 512), BF),
             pltpu.VMEM((1024, 256), BF),
-            pltpu.VMEM((4, 128, 128), F32),
-            pltpu.VMEM((4, 128, 128), F32),
+            pltpu.VMEM((4, 128, 128), BF),
+            pltpu.VMEM((4, 128, 128), BF),
             pltpu.VMEM((16, 8, 128), F32),
             pltpu.VMEM((16, 8, 128), F32),
             pltpu.VMEM((64, 128), jnp.int32),
@@ -379,15 +373,15 @@
             pltpu.SMEM((64, 128), jnp.int32),
             pltpu.SMEM((3, 16, 128), jnp.int32),
             dma((16,)),
-            dma((2, HALF, SUB)), dma((2, HALF, SUB)),
-            dma((7,)), dma((7,)),
-            dma((7,)), dma((7,)),
-            dma((7,)), dma((7,)),
+            dma((2,)), dma((2, HALF, SUB)),
+            dma((1,)), dma((1,)),
+            dma((1,)), dma((1,)),
+            dma((1,)), dma((1,)),
             dma((2,)), dma((2,)),
             dma((3,)), dma((3,)),
-            dma((3, 16)), dma((3, 16)),
             dma((3,)), dma((3,)),
-            dma((16,)), dma((16,)),
+            dma((4,)), dma((4,)),
+            dma((1,)), dma((1,)),
         ],
         compiler_params=pltpu.CompilerParams(
             collective_id=0, has_side_effects=True, vmem_limit_bytes=60 * 1024 * 1024

time: 80.6 us -> 77 us (0.955)
  the two profiles are of different devices: /device:TPU:16 before, /device:TPU:2 now
where the time goes in v3:
time: 77 us; the launch traced here: 76.8 us
  Pallas kernels  74 us (96%)
  local copies, waits for them, and re-layouts  2.18 us (3%)
    pallas_call x1, Pallas kernels, local(): pl.pallas_call(kernel, out_shape=(jax.ShapeDtypeStruct((128, 512), BF), j...  74 us
    unnamed x4, local copies, waits for them, and re-layouts  2.18 us

profile of v3, /device:TPU:2, one launch (start us, length us, event | category | flops | bytes accessed | tf_op | source)
XLA Modules:
  0.0 76.8 jit_solution(5218637675844802600)
XLA Ops:
  0.6 74.0 %shard_map.77 = (bf16[128,512]{1,0:T(8,128)(2,1)}, f32[2,8,64]{2,1,0:T(8,128)}) custom-call(s32[2,8]{1,0:T(2,128)} %bitcast.3, bf16[64,1024]{1,0:T(8,128)(2,1)} %bitcast.2, bf16[8,2,128,128]{3,2,1,0:T(8,128)(2,1)} %adj_hbm.1, bf16[512,512]{1,0:T(8,128)(2,1)} %ws_hbm.1, bf16[512,512]{1,0:T(8,128)(2,1)} %wn_hbm.1, bf16[128,512]{1,0:T(8,128)(2,1)} %cot_hbm.1), custom_call_target="tpu_custom_call" | custom-call | flops 500000000 | bytes 2500000 | tf_op jit(solution)/shard_map/pallas_call | solution.py:342
  74.6 0.0 copy-start
  74.7 1.6 %copy.10 = bf16[128,512]{1,0:T(8,128)(2,1)} copy(bf16[128,512]{1,0:T(8,128)(2,1)} %get-tuple-element.4) | data formatting | bytes 262144
  76.2 0.0 copy-done
  76.2 0.6 copy.11
Async XLA Ops:
  74.6 1.6 %copy-start = (f32[2,8,64]{2,1,0:T(8,128)S(1)}, f32[2,8,64]{2,1,0:T(8,128)}, u32[]{:S(2)}) copy-start(f32[2,8,64]{2,1,0:T(8,128)} %get-tuple-element.5) | copy-start | bytes 12292

commit v4 on v3

--- a/solution.py
+++ b/solution.py
@@ -174,19 +174,26 @@
                 picked[k - 1, chunk, rank] = hold[asked_s[k - 1, chunk, rank]]
             use_copy(k, chunk).start()
 
-    ask_smem.wait()
-    send_uses(z)
-
-    def ring_step(step, carry):
-        for piece in range(SUB):
+    def forward(step, pieces):
+        for piece in pieces:
             for way in range(2):
                 arriving(way, step - 1, piece).wait_recv()
                 sent(way, step, piece).start()
+
+    forward(1, range(SUB // 2))
+    ask_smem.wait()
+    send_uses(z)
+    forward(1, range(SUB // 2, SUB))
+    for way in range(2):
+        send_uses(turn(z, -1 if way == 0 else 1, Z))
+
+    def ring_step(step, carry):
+        forward(step, range(SUB))
         for way in range(2):
             send_uses(turn(z, -step if way == 0 else step, Z))
         return carry
 
-    lax.fori_loop(1, HALF - 1, ring_step, 0)
+    lax.fori_loop(2, HALF - 1, ring_step, 0)
     for piece in range(SUB):
         for way in range(2):
             arriving(way, HALF - 2, piece).wait_recv()
@@ -228,11 +235,11 @@
     pre_self[...] = dot(own_f[...], ws[...], 0, 0)
     for k in range(1, Y):
         all_uses(k).wait_recv()
-    def use(u):
-        block = nb_s[u // 8, u % 8]
+    def use(k, b):
+        block = nb_s[k, b]
         owner = block // 8
         ahead = lax.rem(owner // Z - y + Y, Y)
-        rank = jnp.where(table_s[owner, 2] == u, 0, 1)
+        rank = jnp.where(table_s[owner, 2] == 8 * k + b, 0, 1)
         other = used[jnp.maximum(ahead, 1) - 1, lax.rem(owner, Z), rank]
         return jnp.where(ahead == 0, zbuf[lax.rem(block, 8 * Z)], other)
 
@@ -243,38 +250,47 @@
             as_.at[0], ar.at[0], in_rep(q),
         )
 
-    for b in range(8):
-        raw = dot(use(b), adj[b, 0], 1, 1) + dot(use(8 + b), adj[b, 1], 1, 1)
+    for k in (4, 3, 5, 2, 6, 1, 7, 0):
+        b = turn(rep, k, REP)
+        raw = dot(use(0, b), adj[b, 0], 1, 1) + dot(use(1, b), adj[b, 1], 1, 1)
         agg = (raw * scale[b, 0:1, :]).astype(BF)
-        lhs[mine_a, pl.ds(128 * b, 128)] = agg
-    for k in range(1, REP):
-        agg_copy(k, turn(rep, k, REP), rep).start()
+        lhs[mine_a, pl.ds(pl.multiple_of(128 * b, 128), 128)] = agg
+        if k:
+            agg_copy(k, b, rep).start()
+        else:
+            own_a[own_rows] = agg
     some_a = own_a.at[pl.ds(0, 448)]
     all_a = remote(some_a, some_a, as_.at[0], ar.at[0], in_rep(turn(rep, 1, REP)))
     pair_a = remote(lhs.at[mine_a], lhs.at[mine_a], ps.at[1], pr.at[1], pair)
     go(pair_a)
     finish()
-    own_a[own_rows] = lhs[mine_a, pl.ds(pl.multiple_of(rep * 128, 128), 128)]
     later[3].wait()
     later[4].wait()
     all_a.wait_recv()
     ends.append(all_a.wait_send)
 
-    pre = pre_self[...] + dot(own_a[...], wn[...], 0, 0)
-    s = 1.0 / (1.0 + jnp.exp(-pre))
-    out_ref[...] = (pre * s).astype(BF)
-    g_own[...] = (cot[...].astype(F32) * (s * (1.0 + pre * (1.0 - s)))).astype(BF)
-
 
     def g_copy(k, q, source):
         return remote(
-            g_own.at[:, pl.ds(pl.multiple_of(lax.rem(q, 2) * 256, 256), 256)],
+            g_own.at[:, pl.ds(256 * (k % 2), 256)],
             g_all.at[pl.ds(pl.multiple_of(source * 128, 128), 128)],
             gs.at[0], gr.at[0], in_rep(q),
         )
 
-    for k in (4, 3, 5, 2, 6, 1, 7):
-        g_copy(k, turn(rep, k, REP), rep).start()
+    for half in range(2):
+        cols = slice(256 * half, 256 * half + 256)
+        pre = pre_self[:, cols] + dot(own_a[...], wn[:, cols], 0, 0)
+        s = 1.0 / (1.0 + jnp.exp(-pre))
+        g_own[:, cols] = (cot[:, cols].astype(F32) * (s * (1.0 + pre * (1.0 - s)))).astype(BF)
+        out_ref[:, cols] = (pre * s).astype(BF)
+        for step in (2, 1, 3):
+            chip = turn(x, step, X)
+            g_copy(2 * step + half, 2 * chip + half, rep).start()
+
+        @pl.when(core != half)
+        def _():
+            g_copy(half, 2 * x + half, rep).start()
+
     some_g = g_all.at[pl.ds(0, 896)]
     all_g = remote(some_g, some_g, gs.at[0], gr.at[0], in_rep(turn(rep, 1, REP)))
     g_all[pl.ds(pl.multiple_of(rep * 128, 128), 128)] = g_own[

time: 77 us -> 75.4 us (0.979)
  the two profiles are of different devices: /device:TPU:2 before, /device:TPU:6 now
where the time goes in v4:
time: 75.4 us; the launch traced here: 75.2 us
  Pallas kernels  72.4 us (96%)
  local copies, waits for them, and re-layouts  2.18 us (3%)
    pallas_call x1, Pallas kernels, local(): pl.pallas_call(kernel, out_shape=(jax.ShapeDtypeStruct((128, 512), BF), j...  72.4 us
    unnamed x4, local copies, waits for them, and re-layouts  2.18 us

profile of v4, /device:TPU:6, one launch (start us, length us, event | category | flops | bytes accessed | tf_op | source)
XLA Modules:
  0.0 75.2 jit_solution(15840790878361365509)
XLA Ops:
  0.6 72.4 %shard_map.77 = (bf16[128,512]{1,0:T(8,128)(2,1)}, f32[2,8,64]{2,1,0:T(8,128)}) custom-call(s32[2,8]{1,0:T(2,128)} %bitcast.3, bf16[64,1024]{1,0:T(8,128)(2,1)} %bitcast.2, bf16[8,2,128,128]{3,2,1,0:T(8,128)(2,1)} %adj_hbm.1, bf16[512,512]{1,0:T(8,128)(2,1)} %ws_hbm.1, bf16[512,512]{1,0:T(8,128)(2,1)} %wn_hbm.1, bf16[128,512]{1,0:T(8,128)(2,1)} %cot_hbm.1), custom_call_target="tpu_custom_call" | custom-call | flops 500000000 | bytes 2500000 | tf_op jit(solution)/shard_map/pallas_call | solution.py:358
  73.0 0.0 copy-start
  73.0 1.6 %copy.10 = bf16[128,512]{1,0:T(8,128)(2,1)} copy(bf16[128,512]{1,0:T(8,128)(2,1)} %get-tuple-element.4) | data formatting | bytes 262144
  74.6 0.0 copy-done
  74.6 0.6 copy.11
Async XLA Ops:
  73.0 1.6 %copy-start = (f32[2,8,64]{2,1,0:T(8,128)S(1)}, f32[2,8,64]{2,1,0:T(8,128)}, u32[]{:S(2)}) copy-start(f32[2,8,64]{2,1,0:T(8,128)} %get-tuple-element.5) | copy-start | bytes 12292

commit v5 on v4

--- a/solution.py
+++ b/solution.py
@@ -19,10 +19,10 @@
 
 
 def kernel(
-    nb_ref, f_hbm, adj_hbm, ws_hbm, wn_hbm, cot_hbm,
+    nb_hbm, f_hbm, adj_hbm, ws_hbm, wn_hbm, cot_hbm,
     out_ref, wg_ref,
     zbuf, hold, picked, used, own_f, own_a, lhs, adj, ws, wn, cot,
-    scale, pre_self, g_own, g_all, parts, y_in, y_sum, z_in, table, asked, nb_s, table_s, asked_s,
+    scale, pre_self, g_own, g_all, parts, y_in, y_sum, z_in, table, asked, nb_v, nb_s, table_s, asked_s,
     load_sem, zs, zr, fs, fr, as_, ar, gs, gr, ps, pr, ns, nr, ys, yr, ts, tr, us, ur,
 ):
     row, rep = lax.axis_index("rows"), lax.axis_index("rep")
@@ -72,7 +72,9 @@
         pltpu.make_async_copy(wn_hbm, wn, load_sem.at[11]),
         pltpu.make_async_copy(cot_hbm, cot, load_sem.at[12]),
     ]
-    for c in first + later:
+    numbers = pltpu.make_async_copy(nb_hbm, nb_v, load_sem.at[16])
+    numbers.start()
+    for c in first:
         c.start()
 
     barrier = pltpu.get_barrier_semaphore()
@@ -86,12 +88,15 @@
         pl.semaphore_signal(
             barrier, inc=1, device_id=in_rep(turn(rep, k, REP)), device_id_type=MESH
         )
+    for c in later:
+        c.start()
+    numbers.wait()
     owner_id = lax.broadcasted_iota(jnp.int32, (64, 8), 0)
     lane = lax.broadcasted_iota(jnp.int32, (64, 8), 1)
     low = jnp.full((64, 1), 255, jnp.int32)
     high = jnp.zeros((64, 1), jnp.int32)
     for k in range(2):
-        block = nb_ref[k : k + 1, :]
+        block = nb_v[k : k + 1, :]
         named = block // 8 == owner_id
         code = (8 * k + lane) * 8 + block % 8
         low = jnp.minimum(low, jnp.min(jnp.where(named, code, 255), axis=1, keepdims=True))
@@ -99,7 +104,7 @@
     lane = lax.broadcasted_iota(jnp.int32, (64, 128), 1)
     table[...] = jnp.where(lane == 0, low % 8, jnp.where(lane == 1, high % 8, low // 8))
     to_smem = [
-        pltpu.make_async_copy(nb_ref, nb_s, load_sem.at[13]),
+        pltpu.make_async_copy(nb_v, nb_s, load_sem.at[13]),
         pltpu.make_async_copy(table, table_s, load_sem.at[14]),
     ]
     for c in to_smem:
@@ -115,26 +120,28 @@
             in_rows(yy, z),
         )
 
+
+    def ring_copy(way, step, piece, chunk):
+        at = pl.ds(chunk * 8 + piece * PIECE, PIECE)
+        return remote(
+            zbuf.at[at], zbuf.at[at], zs.at[way], zr.at[way, step, piece],
+            right if way == 0 else left,
+        )
+
+    def sent(way, step, piece):
+        return ring_copy(way, step, piece, turn(z, -step if way == 0 else step, Z))
+
+    def arriving(way, step, piece):
+        return ring_copy(way, step, piece, turn(z, -1 - step if way == 0 else 1 + step, Z))
+
+    def last_way(piece):
+        return 0 if piece < SUB // 2 else 1
+
+    for way in range(2):
+        sent(way, 0, 0).start()
     for k in (2, 1, 3):
         go(table_copy(k))
-
-    def ring_copy(way, step, piece, chunk):
-        at = pl.ds(chunk * 8 + piece * PIECE, PIECE)
-        return remote(
-            zbuf.at[at], zbuf.at[at], zs.at[way], zr.at[way, step, piece],
-            right if way == 0 else left,
-        )
-
-    def sent(way, step, piece):
-        return ring_copy(way, step, piece, turn(z, -step if way == 0 else step, Z))
-
-    def arriving(way, step, piece):
-        return ring_copy(way, step, piece, turn(z, -1 - step if way == 0 else 1 + step, Z))
-
-    def last_way(piece):
-        return 0 if piece < SUB // 2 else 1
-
-    for piece in range(SUB):
+    for piece in range(1, SUB):
         for way in range(2):
             sent(way, 0, piece).start()
 
@@ -361,7 +368,7 @@
             jax.ShapeDtypeStruct((128, 512), BF),
             jax.ShapeDtypeStruct((2, 8, 64), F32),
         ),
-        in_specs=[vmem] + [anywhere] * 5,
+        in_specs=[anywhere] * 6,
         out_specs=(vmem, vmem),
         scratch_shapes=[
             pltpu.VMEM((128, 64, 128), BF),
@@ -385,10 +392,11 @@
             pltpu.VMEM((16, 8, 128), F32),
             pltpu.VMEM((64, 128), jnp.int32),
             pltpu.VMEM((3, 16, 128), jnp.int32),
+            pltpu.VMEM((2, 8), jnp.int32),
             pltpu.SMEM((2, 8), jnp.int32),
             pltpu.SMEM((64, 128), jnp.int32),
             pltpu.SMEM((3, 16, 128), jnp.int32),
-            dma((16,)),
+            dma((17,)),
             dma((2,)), dma((2, HALF, SUB)),
             dma((1,)), dma((1,)),
             dma((1,)), dma((1,)),

time: 75.4 us -> 74.8 us (level)
  no operation moved by 1% of the time
where the time goes in v5:
time: 74.8 us; the launch traced here: 74.6 us
  Pallas kernels  71.8 us (96%)
  local copies, waits for them, and re-layouts  2.18 us (3%)
    pallas_call x1, Pallas kernels, local(): pl.pallas_call(kernel, out_shape=(jax.ShapeDtypeStruct((128, 512), BF), j...  71.8 us
    unnamed x4, local copies, waits for them, and re-layouts  2.18 us

profile of v5, /device:TPU:6, one launch (start us, length us, event | category | flops | bytes accessed | tf_op | source)
XLA Modules:
  0.0 74.6 jit_solution(13299136338503124033)
XLA Ops:
  0.6 71.8 %shard_map.77 = (bf16[128,512]{1,0:T(8,128)(2,1)}, f32[2,8,64]{2,1,0:T(8,128)}) custom-call(s32[2,8]{1,0:T(2,128)} %bitcast.3, bf16[64,1024]{1,0:T(8,128)(2,1)} %bitcast.2, bf16[8,2,128,128]{3,2,1,0:T(8,128)(2,1)} %adj_hbm.1, bf16[512,512]{1,0:T(8,128)(2,1)} %ws_hbm.1, bf16[512,512]{1,0:T(8,128)(2,1)} %wn_hbm.1, bf16[128,512]{1,0:T(8,128)(2,1)} %cot_hbm.1), custom_call_target="tpu_custom_call" | custom-call | flops 500000000 | bytes 2500000 | tf_op jit(solution)/shard_map/pallas_call | solution.py:365
  72.4 0.0 copy-start
  72.5 1.6 %copy.10 = bf16[128,512]{1,0:T(8,128)(2,1)} copy(bf16[128,512]{1,0:T(8,128)(2,1)} %get-tuple-element.4) | data formatting | bytes 262144
  74.0 0.0 copy-done
  74.0 0.6 copy.11
Async XLA Ops:
  72.4 1.6 %copy-start = (f32[2,8,64]{2,1,0:T(8,128)S(1)}, f32[2,8,64]{2,1,0:T(8,128)}, u32[]{:S(2)}) copy-start(f32[2,8,64]{2,1,0:T(8,128)} %get-tuple-element.5) | copy-start | bytes 12292

commit v6 on v5

--- a/solution.py
+++ b/solution.py
@@ -287,7 +287,7 @@
     for half in range(2):
         cols = slice(256 * half, 256 * half + 256)
         pre = pre_self[:, cols] + dot(own_a[...], wn[:, cols], 0, 0)
-        s = 1.0 / (1.0 + jnp.exp(-pre))
+        s = jax.nn.sigmoid(pre)
         g_own[:, cols] = (cot[:, cols].astype(F32) * (s * (1.0 + pre * (1.0 - s)))).astype(BF)
         out_ref[:, cols] = (pre * s).astype(BF)
         for step in (2, 1, 3):

time: 74.8 us -> 74.8 us (level)
  no operation moved by 1% of the time
where the time goes in v6:
time: 74.8 us; the launch traced here: 74.6 us
  Pallas kernels  71.8 us (96%)
  local copies, waits for them, and re-layouts  2.18 us (3%)
    pallas_call x1, Pallas kernels, local(): pl.pallas_call(kernel, out_shape=(jax.ShapeDtypeStruct((128, 512), BF), j...  71.8 us
    unnamed x4, local copies, waits for them, and re-layouts  2.18 us

profile of v6, /device:TPU:6, one launch (start us, length us, event | category | flops | bytes accessed | tf_op | source)
XLA Modules:
  0.0 74.6 jit_solution(15624291043092603184)
XLA Ops:
  0.6 71.8 %shard_map.77 = (bf16[128,512]{1,0:T(8,128)(2,1)}, f32[2,8,64]{2,1,0:T(8,128)}) custom-call(s32[2,8]{1,0:T(2,128)} %bitcast.3, bf16[64,1024]{1,0:T(8,128)(2,1)} %bitcast.2, bf16[8,2,128,128]{3,2,1,0:T(8,128)(2,1)} %adj_hbm.1, bf16[512,512]{1,0:T(8,128)(2,1)} %ws_hbm.1, bf16[512,512]{1,0:T(8,128)(2,1)} %wn_hbm.1, bf16[128,512]{1,0:T(8,128)(2,1)} %cot_hbm.1), custom_call_target="tpu_custom_call" | custom-call | flops 500000000 | bytes 2500000 | tf_op jit(solution)/shard_map/pallas_call | solution.py:365
  72.4 0.0 copy-start
  72.4 1.6 %copy.10 = bf16[128,512]{1,0:T(8,128)(2,1)} copy(bf16[128,512]{1,0:T(8,128)(2,1)} %get-tuple-element.4) | data formatting | bytes 262144
  74.0 0.0 copy-done
  74.0 0.6 copy.11
Async XLA Ops:
  72.4 1.6 %copy-start = (f32[2,8,64]{2,1,0:T(8,128)S(1)}, f32[2,8,64]{2,1,0:T(8,128)}, u32[]{:S(2)}) copy-start(f32[2,8,64]{2,1,0:T(8,128)} %get-tuple-element.5) | copy-start | bytes 12292

commit v7 on v6

--- a/solution.py
+++ b/solution.py
@@ -259,7 +259,8 @@
 
     for k in (4, 3, 5, 2, 6, 1, 7, 0):
         b = turn(rep, k, REP)
-        raw = dot(use(0, b), adj[b, 0], 1, 1) + dot(use(1, b), adj[b, 1], 1, 1)
+        both = jnp.concatenate([use(0, b), use(1, b)], axis=1)
+        raw = dot(both, jnp.concatenate([adj[b, 0], adj[b, 1]], axis=1), 1, 1)
         agg = (raw * scale[b, 0:1, :]).astype(BF)
         lhs[mine_a, pl.ds(pl.multiple_of(128 * b, 128), 128)] = agg
         if k:

time: 74.8 us -> 74.6 us (level)
  no operation moved by 1% of the time
where the time goes in v7:
time: 74.6 us; the launch traced here: 74.5 us
  Pallas kernels  71.7 us (96%)
  local copies, waits for them, and re-layouts  2.18 us (3%)
    pallas_call x1, Pallas kernels, local(): pl.pallas_call(kernel, out_shape=(jax.ShapeDtypeStruct((128, 512), BF), j...  71.7 us
    unnamed x4, local copies, waits for them, and re-layouts  2.18 us

profile of v7, /device:TPU:6, one launch (start us, length us, event | category | flops | bytes accessed | tf_op | source)
XLA Modules:
  0.0 74.5 jit_solution(15116592590925129035)
XLA Ops:
  0.6 71.7 %shard_map.77 = (bf16[128,512]{1,0:T(8,128)(2,1)}, f32[2,8,64]{2,1,0:T(8,128)}) custom-call(s32[2,8]{1,0:T(2,128)} %bitcast.3, bf16[64,1024]{1,0:T(8,128)(2,1)} %bitcast.2, bf16[8,2,128,128]{3,2,1,0:T(8,128)(2,1)} %adj_hbm.1, bf16[512,512]{1,0:T(8,128)(2,1)} %ws_hbm.1, bf16[512,512]{1,0:T(8,128)(2,1)} %wn_hbm.1, bf16[128,512]{1,0:T(8,128)(2,1)} %cot_hbm.1), custom_call_target="tpu_custom_call" | custom-call | flops 500000000 | bytes 2500000 | tf_op jit(solution)/shard_map/pallas_call | solution.py:366
  72.3 0.0 copy-start
  72.3 1.6 %copy.10 = bf16[128,512]{1,0:T(8,128)(2,1)} copy(bf16[128,512]{1,0:T(8,128)(2,1)} %get-tuple-element.4) | data formatting | bytes 262144
  73.9 0.0 copy-done
  73.9 0.6 copy.11
Async XLA Ops:
  72.3 1.6 %copy-start = (f32[2,8,64]{2,1,0:T(8,128)S(1)}, f32[2,8,64]{2,1,0:T(8,128)}, u32[]{:S(2)}) copy-start(f32[2,8,64]{2,1,0:T(8,128)} %get-tuple-element.5) | copy-start | bytes 12292

commit v8 on v6

--- a/solution.py
+++ b/solution.py
@@ -20,9 +20,9 @@
 
 def kernel(
     nb_hbm, f_hbm, adj_hbm, ws_hbm, wn_hbm, cot_hbm,
-    out_ref, wg_ref,
+    out_hbm, wg_ref,
     zbuf, hold, picked, used, own_f, own_a, lhs, adj, ws, wn, cot,
-    scale, pre_self, g_own, g_all, parts, y_in, y_sum, z_in, table, asked, nb_v, nb_s, table_s, asked_s,
+    scale, pre_self, g_own, g_all, parts, y_in, y_sum, z_in, table, asked, nb_v, nb_s, table_s, asked_s, out_v,
     load_sem, zs, zr, fs, fr, as_, ar, gs, gr, ps, pr, ns, nr, ys, yr, ts, tr, us, ur,
 ):
     row, rep = lax.axis_index("rows"), lax.axis_index("rep")
@@ -289,7 +289,7 @@
         pre = pre_self[:, cols] + dot(own_a[...], wn[:, cols], 0, 0)
         s = jax.nn.sigmoid(pre)
         g_own[:, cols] = (cot[:, cols].astype(F32) * (s * (1.0 + pre * (1.0 - s)))).astype(BF)
-        out_ref[:, cols] = (pre * s).astype(BF)
+        out_v[:, cols] = (pre * s).astype(BF)
         for step in (2, 1, 3):
             chip = turn(x, step, X)
             g_copy(2 * step + half, 2 * chip + half, rep).start()
@@ -298,6 +298,8 @@
         def _():
             g_copy(half, 2 * x + half, rep).start()
 
+    write = pltpu.make_async_copy(out_v, out_hbm, load_sem.at[17])
+    write.start()
     some_g = g_all.at[pl.ds(0, 896)]
     all_g = remote(some_g, some_g, gs.at[0], gr.at[0], in_rep(turn(rep, 1, REP)))
     g_all[pl.ds(pl.multiple_of(rep * 128, 128), 128)] = g_own[
@@ -357,6 +359,7 @@
     wg_ref[0] = grads[:, :64]
     wg_ref[1] = grads[:, 64:]
     all_z.wait_send()
+    write.wait()
 
 
 def local(features, neighbor_blocks, adjacency, w_self, w_neigh, cotangent):
@@ -369,7 +372,7 @@
             jax.ShapeDtypeStruct((2, 8, 64), F32),
         ),
         in_specs=[anywhere] * 6,
-        out_specs=(vmem, vmem),
+        out_specs=(anywhere, vmem),
         scratch_shapes=[
             pltpu.VMEM((128, 64, 128), BF),
             pltpu.VMEM((8, 64, 128), BF),
@@ -396,7 +399,8 @@
             pltpu.SMEM((2, 8), jnp.int32),
             pltpu.SMEM((64, 128), jnp.int32),
             pltpu.SMEM((3, 16, 128), jnp.int32),
-            dma((17,)),
+            pltpu.VMEM((128, 512), BF),
+            dma((18,)),
             dma((2,)), dma((2, HALF, SUB)),
             dma((1,)), dma((1,)),
             dma((1,)), dma((1,)),

time: 74.8 us -> 74.7 us (level)
  no operation moved by 1% of the time
where the time goes in v8:
time: 74.7 us; the launch traced here: 74.6 us
  Pallas kernels  71.8 us (96%)
  local copies, waits for them, and re-layouts  2.18 us (3%)
    pallas_call x1, Pallas kernels, local(): pl.pallas_call(kernel, out_shape=(jax.ShapeDtypeStruct((128, 512), BF), j...  71.8 us
    unnamed x4, local copies, waits for them, and re-layouts  2.18 us

profile of v8, /device:TPU:6, one launch (start us, length us, event | category | flops | bytes accessed | tf_op | source)
XLA Modules:
  0.0 74.6 jit_solution(9648313220131604315)
XLA Ops:
  0.6 71.8 %shard_map.77 = (bf16[128,512]{1,0:T(8,128)(2,1)}, f32[2,8,64]{2,1,0:T(8,128)}) custom-call(s32[2,8]{1,0:T(2,128)} %bitcast.3, bf16[64,1024]{1,0:T(8,128)(2,1)} %bitcast.2, bf16[8,2,128,128]{3,2,1,0:T(8,128)(2,1)} %adj_hbm.1, bf16[512,512]{1,0:T(8,128)(2,1)} %ws_hbm.1, bf16[512,512]{1,0:T(8,128)(2,1)} %wn_hbm.1, bf16[128,512]{1,0:T(8,128)(2,1)} %cot_hbm.1), custom_call_target="tpu_custom_call" | custom-call | flops 500000000 | bytes 2500000 | tf_op jit(solution)/shard_map/pallas_call | solution.py:368
  72.4 0.0 copy-start
  72.4 1.6 %copy.10 = bf16[128,512]{1,0:T(8,128)(2,1)} copy(bf16[128,512]{1,0:T(8,128)(2,1)} %get-tuple-element.4) | data formatting | bytes 262144
  74.0 0.0 copy-done
  74.0 0.6 copy.11
Async XLA Ops:
  72.4 1.6 %copy-start = (f32[2,8,64]{2,1,0:T(8,128)S(1)}, f32[2,8,64]{2,1,0:T(8,128)}, u32[]{:S(2)}) copy-start(f32[2,8,64]{2,1,0:T(8,128)} %get-tuple-element.5) | copy-start | bytes 12292
